TPU v7x, 32 devices: a whole 2x2x4 slice. The times are simulated.
32 devices in a mesh: head: 2 (over x), blk: 16 (over z, y, core).
Axes of the slice: x: 2, y: 2, z: 4, core: 2. Of those that a mesh axis runs over, the one named last changes fastest.
Arguments:
- queries: bfloat16 [2, 6144, 5120], P('head', 'blk'), may hold values from -8 to 8
- keys: bfloat16 [2, 6144, 5120], P('head', 'blk'), may hold values from -8 to 8
- values: bfloat16 [2, 6144, 5120], P('head', 'blk'), may hold values from -6 to 6
- q_gain: float32 [5120], replicated, may hold values from 0.1 to 1.9
- k_gain: float32 [5120], replicated, may hold values from 0.1 to 1.9
- slopes: float32 [40], P('head'), may hold values from 0.25 to 4
- out_weight: bfloat16 [5120, 5120], P('head', 'blk'), may hold values from -1 to 1
- kv_tiles: int32 [32, 4], replicated, may hold values from 0 to 31, as said below
- tile_frame: int32 [32], replicated, may hold values from 0 to 3, never falling along the last dimension, each value on 1 to 16 neighbouring positions
Outputs:
- mixed: bfloat16 [2, 6144, 5120], P('head', 'blk')
Inputs may be any that keep to these rules, and one draw needn't show every extreme that they name: kv_tiles[t, 0] = t; the other entries of row t are distinct tiles other than t, each within 3 tiles of t. `tile_frame`: never falls from one tile to the next.
All inputs are finite; a program needn't handle non-finite values.
Results may differ from a plain program's by a relative error of at most 0.013.
Values may be sent and summed in bfloat16 or wider, within the bound.
A program may use at most 256 MiB of HBM per device.

v0:
```python
import math

import jax
import jax.numpy as jnp
from jax import lax
from jax.experimental import pallas as pl
from jax.experimental.pallas import tpu as pltpu
from jax.sharding import PartitionSpec as P

HDIM = 128
TILE = 384
REACH = 3
LOG2E = math.log2(math.e)
CHUNKS = 4
TEAM = 8
STEP = 2
LINE = 4
PIECES = 5
NORM_ROWS = 64
NORM_GROUP = 16
MESH = pl.DeviceIdType.MESH
FLIPS = ((1, 0, 0), (0, 1, 0), (1, 0, 1), (0, 1, 1), (1, 1, 0), (1, 1, 1), (0, 0, 1))
VMEM_LIMIT = 60 * 1024 * 1024


def fused_kernel(sizes, index_ref, penalty_ref, q_gain_ref, k_gain_ref, q_ref, k_ref, v_ref, w_ref, out_ref, *scratch):
    planes, hpd, length, pair = sizes
    wins = REACH + 1
    slabs = TEAM * hpd
    per_tile = pair // HDIM
    frame = w_ref.shape[1]
    base = frame - HDIM
    inner = w_ref.shape[0]
    key_wins, value_wins = scratch[:hpd], scratch[hpd : 2 * hpd]
    (queries, keys_n, queries_n, gathered, weight, arrived, raw) = scratch[2 * hpd : 2 * hpd + 7]
    (
        raw_sem,
        qkv_send,
        qkv_recv,
        qkv_local,
        halo_send,
        halo_recv,
        w_send,
        w_recv,
        w_local,
        att_send,
        att_recv,
        att_local,
        x_send,
        x_recv,
        y_send,
        y_recv,
        out_local,
    ) = scratch[2 * hpd + 7 :]

    x, b = lax.axis_index("head"), lax.axis_index("blk")
    z, m = b // LINE, b % LINE
    y, c = m // 2, m % 2
    me = m * 2 + x

    def device(xx, zz, mm):
        return (xx, zz * LINE + mm)

    def remote(src, dst, send, recv, target):
        copy = pltpu.make_async_remote_copy(
            src_ref=src, dst_ref=dst, send_sem=send, recv_sem=recv, device_id=target, device_id_type=MESH
        )
        copy.start()

    def local(src, dst, sem):
        pltpu.make_async_copy(src, dst, sem).start()

    def wait(like, sem):
        pltpu.make_async_copy(like, like, sem).wait()

    def lanes(at):
        return pl.ds(pl.multiple_of(at * HDIM, HDIM), HDIM)

    mates = []
    for dx, dy, dc in FLIPS:
        mates.append(((x + dx) % 2, ((y + dy) % 2) * 2 + (c + dc) % 2))
    planes_off = [(z + k) % planes for k in range(1, planes)]

    barrier = pltpu.get_barrier_semaphore()
    for xx, mm in mates:
        pl.semaphore_signal(barrier, inc=1, device_id=device(xx, z, mm), device_id_type=MESH)
    for zz in planes_off:
        pl.semaphore_signal(barrier, inc=1, device_id=device(x, zz, m), device_id_type=MESH)
    pl.semaphore_wait(barrier, len(mates) + len(planes_off))

    rail = pl.ds(pl.multiple_of(c * frame, HDIM), frame)
    sibling = device(x, z, y * 2 + 1 - c)

    def weight_piece(piece):
        rows = pl.ds(piece * (inner // PIECES), inner // PIECES)
        for k, zz in enumerate(planes_off):
            remote(w_ref.at[rows], weight.at[z, rows, rail], w_send.at[k], w_recv.at[z * 2 + c], device(x, zz, m))

    def weight_forward(zz):
        wait(weight.at[zz, :, rail], w_recv.at[zz * 2 + c])
        remote(weight.at[zz, :, rail], weight.at[zz, :, rail], w_send.at[planes], w_recv.at[zz * 2 + c], sibling)

    local(w_ref, weight.at[z, :, rail], w_local)
    remote(w_ref, weight.at[z, :, rail], w_send.at[planes - 1], w_recv.at[z * 2 + c], sibling)

    def scatter(kind, h, source, window, at):
        for xx, mm in mates:
            head = (xx * LINE + mm) * hpd + h
            remote(source(head), window.at[at], qkv_send.at[kind], qkv_recv.at[kind, h], device(xx, z, mm))
        local(source((x * LINE + m) * hpd + h), window.at[at], qkv_local.at[kind, h])

    for h in range(hpd):
        scatter(0, h, lambda head: v_ref.at[0, :, lanes(head)], value_wins[h], REACH + me)

    def normed(source, gain_ref, target):
        steps = length // NORM_ROWS

        def chunk(step, slot):
            return pltpu.make_async_copy(
                source.at[0, pl.ds(step * NORM_ROWS, NORM_ROWS)], raw.at[slot], raw_sem.at[slot]
            )

        chunk(0, 0).start()

        @pl.loop(0, steps)
        def _(step):
            slot = step % 2

            @pl.when(step + 1 < steps)
            def _():
                chunk(step + 1, 1 - slot).start()

            chunk(step, slot).wait()

            @pl.loop(0, NORM_ROWS // NORM_GROUP)
            def _(group):
                floats = raw[slot, pl.ds(group * NORM_GROUP, NORM_GROUP), :].astype(jnp.float32)
                factor = lax.rsqrt(jnp.mean(floats * floats, axis=-1, keepdims=True) + 1e-06)
                rows = (floats * factor * gain_ref[...]).astype(jnp.bfloat16)
                at = pl.ds(step * NORM_ROWS + group * NORM_GROUP, NORM_GROUP)
                for slab in range(slabs):
                    target[slab, at, :] = rows[:, slab * HDIM : (slab + 1) * HDIM]

    normed(k_ref, k_gain_ref, keys_n)
    normed(q_ref, q_gain_ref, queries_n)
    for h in range(hpd):
        scatter(1, h, lambda head: keys_n.at[head], key_wins[h], REACH + me)
        scatter(2, h, lambda head: queries_n.at[head], queries.at[h], me)
    weight_piece(0)

    def landed(kind, h, window, first):
        own = window.at[pl.ds(first, TEAM - 1)]
        wait(own, qkv_recv.at[kind, h])
        wait(window.at[first], qkv_local.at[kind, h])

    top = REACH + TEAM

    def spread(kind, h, window):
        landed(kind, h, window, REACH)

        @pl.when(z < planes - 1)
        def _():
            remote(
                window.at[pl.ds(TEAM, REACH)],
                window.at[pl.ds(0, REACH)],
                halo_send.at[kind, 0, h],
                halo_recv.at[kind, 0, h],
                device(x, z + 1, m),
            )

        @pl.when(z > 0)
        def _():
            remote(
                window.at[pl.ds(REACH, REACH)],
                window.at[pl.ds(top, REACH)],
                halo_send.at[kind, 1, h],
                halo_recv.at[kind, 1, h],
                device(x, z - 1, m),
            )

    def halo_landed(h):
        for kind, window in ((0, value_wins[h]), (1, key_wins[h])):

            @pl.when(z > 0)
            def _():
                wait(window.at[pl.ds(0, REACH)], halo_recv.at[kind, 0, h])

            @pl.when(z < planes - 1)
            def _():
                wait(window.at[pl.ds(top, REACH)], halo_recv.at[kind, 1, h])

    def attend(h):
        halo_landed(h)

        @pl.loop(0, TEAM)
        def _(i):
            part, mm = i // LINE, i % LINE
            tile = mm * 2 + (x + 1 - part) % 2
            query = queries[h, tile]
            scores = []
            largest = None
            for win in range(wins):
                near = key_wins[h][index_ref[tile * wins + win]]
                score = lax.dot_general(
                    query, near, (((1,), (1,)), ((), ())), preferred_element_type=jnp.float32
                )
                penalty = penalty_ref[(h * TEAM + tile) * wins + win]
                most = jnp.max(score, axis=-1, keepdims=True) - penalty
                largest = most if largest is None else jnp.maximum(largest, most)
                scores.append((score, penalty))
            total = jnp.zeros((length, 1), jnp.float32)
            summed = jnp.zeros((length, HDIM), jnp.float32)
            for win, (score, penalty) in enumerate(scores):
                share = jnp.exp2(score - (largest + penalty))
                total += jnp.sum(share, axis=-1, keepdims=True)
                summed += jnp.dot(
                    share.astype(jnp.bfloat16),
                    value_wins[h][index_ref[tile * wins + win]],
                    preferred_element_type=jnp.float32,
                )
            queries[h, tile] = (summed / total).astype(jnp.bfloat16)
            there = gathered.at[part * 2 + mm // 2, :, lanes(m * hpd + h)]
            core = mm % 2
            remote(
                queries.at[h, tile], there, att_send.at[0], att_recv.at[part], device(x, z, (1 - y) * 2 + core)
            )

            @pl.when(core == c)
            def _():
                local(queries.at[h, tile], there, att_local.at[part])

            @pl.when(core != c)
            def _():
                remote(queries.at[h, tile], there, att_send.at[1], att_recv.at[part], sibling)

    for h in range(hpd):
        spread(0, h, value_wins[h])
    for piece in range(1, 3):
        weight_piece(piece)
    for h in range(hpd):
        spread(1, h, key_wins[h])
        landed(2, h, queries.at[h], 0)
        if h == 1:
            weight_piece(3)
        if h == 2:
            weight_piece(4)
        if h > 0:
            attend(h - 1)
    attend(hpd - 1)

    wait(keys_n.at[pl.ds(0, (TEAM - 1) * hpd)], qkv_send.at[1])
    wait(queries_n.at[pl.ds(0, (TEAM - 1) * hpd)], qkv_send.at[2])

    def near_plane(k):
        if k == 0:
            return z
        if planes == 4:
            low, high = z % 2, z // 2
            return (high + k // 2) % 2 * 2 + (low + k % 2) % 2
        return (z + k) % planes

    def project(part, row, zz):
        own = gathered[part * 2 + row]
        for start, width in ((0, base), (base, 2 * HDIM), (base + 2 * HDIM, base)):
            product = jnp.dot(own, weight[zz, :, start : start + width], preferred_element_type=jnp.float32)
            if start == base:
                yield base // HDIM, product[:, :HDIM] + product[:, HDIM:]
            else:
                first = start // HDIM if start < base else start // HDIM - 1
                for at in range(width // HDIM):
                    yield first + at, product[:, at * HDIM : (at + 1) * HDIM]

    def attended_landed(part):
        wait(keys_n.at[pl.ds(0, 2 * (LINE - 1) * hpd)], att_recv.at[part])
        wait(keys_n.at[pl.ds(0, 2 * hpd)], att_local.at[part])

    attended_landed(0)
    per_plane = 2 * per_tile
    for k in range(planes):
        zz = near_plane(k)
        if k == 0:
            wait(weight.at[zz, :, rail], w_local)
        else:
            weight_forward(zz)
        rest = pl.ds(pl.multiple_of((1 - c) * frame, HDIM), frame)
        wait(weight.at[zz, :, rest], w_recv.at[zz * 2 + 1 - c])

        @pl.loop(0, 2)
        def _(row):
            for slab, product in project(0, row, zz):
                keys_n[k * per_plane + row * per_tile + slab] = product.astype(jnp.bfloat16)

        remote(
            keys_n.at[pl.ds(k * per_plane, per_plane)],
            arrived.at[k],
            x_send.at[k],
            x_recv.at[k],
            device(1 - x, z, m),
        )

    attended_landed(1)
    for k in range(planes):
        zz = near_plane(k)
        wait(arrived.at[k], x_recv.at[k])

        @pl.loop(0, 2)
        def _(turn):
            row = (turn + 1 - y) % 2
            for slab, product in project(1, row, zz):
                floats = product + arrived[k, row * per_tile + slab].astype(jnp.float32)
                queries_n[k * per_plane + row * per_tile + slab] = floats.astype(jnp.bfloat16)
            for slab in range(per_tile):
                source = queries_n.at[k * per_plane + row * per_tile + slab]
                there = out_ref.at[0, :, lanes((zz * 2 + y) * per_tile + slab)]

                @pl.when(row == y)
                def _():
                    local(source, there, out_local)

                @pl.when(row != y)
                def _():
                    remote(source, there, y_send, y_recv, device(x, z, (1 - y) * 2 + c))

    half = planes * per_tile
    wait(queries_n.at[pl.ds(0, half)], y_recv)
    wait(queries_n.at[pl.ds(0, half)], out_local)
    wait(queries_n.at[pl.ds(0, half)], y_send)
    for k in range(planes):
        wait(arrived.at[k], x_send.at[k])
    wait(keys_n.at[pl.ds(0, (TEAM - 1) * hpd)], qkv_send.at[0])
    wait(keys_n, att_send.at[0])
    wait(keys_n.at[pl.ds(0, LINE * hpd)], att_send.at[1])
    for k in range(planes):
        wait(w_ref, w_send.at[k])
    wait(weight.at[pl.ds(0, planes - 1), :, rail], w_send.at[planes])
    for h in range(hpd):
        for kind, window in ((0, value_wins[h]), (1, key_wins[h])):

            @pl.when(z < planes - 1)
            def _():
                wait(window.at[pl.ds(0, REACH)], halo_send.at[kind, 0, h])

            @pl.when(z > 0)
            def _():
                wait(window.at[pl.ds(0, REACH)], halo_send.at[kind, 1, h])


def fused_shards(queries, keys, values, q_gain, k_gain, slopes, out_weight, kv_tiles, tile_frame):
    blocks = lax.axis_size("blk")
    position = lax.axis_index("blk")
    planes, member = blocks // LINE, lax.rem(position, LINE)
    length, features = values.shape[1:]
    hpd = features // (TEAM * HDIM)
    inner, narrow = out_weight.shape
    pair, frame = 2 * narrow, narrow + HDIM // 2

    start = position // LINE * TEAM
    listed = lax.dynamic_slice_in_dim(kv_tiles, start, TEAM, 0)
    own_frames = lax.dynamic_slice_in_dim(tile_frame, start, TEAM, 0)
    gap = jnp.abs(own_frames[:, None] - jnp.take(tile_frame, listed, axis=0)).astype(jnp.float32)
    own_slopes = lax.dynamic_slice_in_dim(slopes, member * hpd, hpd, 0)
    penalty = (own_slopes * LOG2E)[:, None] * gap.reshape(1, -1)
    index = (listed - (start - REACH)).reshape(-1)

    framed = jnp.where(
        position % 2 == 0,
        jnp.pad(out_weight, ((0, 0), (0, HDIM // 2))),
        jnp.pad(out_weight, ((0, 0), (HDIM // 2, 0))),
    )

    def body(*refs):
        fused_kernel((planes, hpd, length, pair), *refs)

    dma, half = pltpu.SemaphoreType.DMA, jnp.bfloat16
    slabs = TEAM * hpd
    anywhere = pl.BlockSpec(memory_space=pl.ANY)
    smem = pl.BlockSpec(memory_space=pltpu.SMEM)
    vmem = pl.BlockSpec(memory_space=pltpu.VMEM)
    window = pltpu.VMEM((TEAM + 2 * REACH, length, HDIM), half)
    rows = TEAM * length
    return pl.pallas_call(
        body,
        in_specs=[smem, smem, vmem, vmem, anywhere, anywhere, anywhere, anywhere],
        out_specs=anywhere,
        out_shape=jax.ShapeDtypeStruct((1, length, narrow * blocks), half),
        scratch_shapes=[window] * (2 * hpd)
        + [
            pltpu.VMEM((hpd, TEAM, length, HDIM), half),
            pltpu.VMEM((slabs, length, HDIM), half),
            pltpu.VMEM((slabs, length, HDIM), half),
            pltpu.VMEM((4, length, inner), half),
            pltpu.VMEM((planes, inner, 2 * frame), half),
            pltpu.VMEM((planes, 2 * pair // HDIM, length, HDIM), half),
            pltpu.VMEM((2, NORM_ROWS, features), half),
            dma((2,)),
            dma((3,)),
            dma((3, hpd)),
            dma((3, hpd)),
            dma((2, 2, hpd)),
            dma((2, 2, hpd)),
            dma((planes + 1,)),
            dma((2 * planes,)),
            dma,
            dma((2,)),
            dma((2,)),
            dma((2,)),
            dma((planes,)),
            dma((planes,)),
            dma,
            dma,
            dma,
        ],
        compiler_params=pltpu.CompilerParams(
            vmem_limit_bytes=VMEM_LIMIT, collective_id=0, has_side_effects=True
        ),
        cost_estimate=pl.CostEstimate(
            flops=4 * rows * (REACH + 1) * TILE * hpd * HDIM + 4 * length * inner * narrow * blocks,
            bytes_accessed=8 * length * features + 2 * inner * narrow,
            transcendentals=rows * (REACH + 1) * TILE * hpd,
        ),
    )(
        index,
        penalty.reshape(-1),
        (q_gain * (LOG2E * HDIM ** (-0.5)))[None],
        k_gain[None],
        queries,
        keys,
        values,
        framed,
    )


def shifted(value, axis, steps):
    count = lax.axis_size(axis)
    initial, last = (max(0, -steps), min(count, count - steps))
    return lax.ppermute(value, axis, [(source, source + steps) for source in range(initial, last)])


def rms_norm(rows, gain):
    floats = rows.astype(jnp.float32)
    factor = lax.rsqrt(jnp.mean(floats * floats, axis=-1, keepdims=True) + 1e-06)
    return (floats * factor * gain).astype(jnp.bfloat16)


def attend_kernel(tiles, wins, parts, index_ref, penalty_ref, *refs):
    q_ref = refs[0]
    key_refs = refs[1 : 1 + parts]
    value_refs = refs[1 + parts : 1 + 2 * parts]
    out_ref, key_window, value_window = refs[1 + 2 * parts :]
    head = pl.program_id(0)
    first = pl.program_id(1) * STEP

    @pl.when(first == 0)
    def _():
        for window, blocks in ((key_window, key_refs), (value_window, value_refs)):
            at = 0
            for block in blocks:
                for tile in range(block.shape[0] // TILE):
                    window[at] = block[tile * TILE : (tile + 1) * TILE, :]
                    at += 1

    for step in range(STEP):
        tile = first + step
        query = q_ref[step * TILE : (step + 1) * TILE, :]
        scores = []
        largest = None
        for win in range(wins):
            near = key_window[index_ref[tile * wins + win]]
            score = lax.dot_general(
                query, near, (((1,), (1,)), ((), ())), preferred_element_type=jnp.float32
            )
            penalty = penalty_ref[(head * tiles + tile) * wins + win]
            top = jnp.max(score, axis=-1, keepdims=True) - penalty
            largest = top if largest is None else jnp.maximum(largest, top)
            scores.append((score, penalty))
        total = jnp.zeros((TILE, 1), jnp.float32)
        summed = jnp.zeros((TILE, HDIM), jnp.float32)
        for win, (score, penalty) in enumerate(scores):
            weight = jnp.exp2(score - (largest + penalty))
            total += jnp.sum(weight, axis=-1, keepdims=True)
            summed += jnp.dot(
                weight.astype(jnp.bfloat16),
                value_window[index_ref[tile * wins + win]],
                preferred_element_type=jnp.float32,
            )
        out_ref[step * TILE : (step + 1) * TILE, :] = (summed / total).astype(out_ref.dtype)


def attend(query, key_parts, value_parts, index, penalty):
    rows, width = query.shape
    heads, tiles, wins = width // HDIM, rows // TILE, index.shape[0] * TILE // rows
    window = sum(part.shape[0] for part in key_parts) // TILE

    def column(array):
        return pl.BlockSpec((array.shape[0], HDIM), lambda h, t, *_: (0, h))

    stepped = pl.BlockSpec((STEP * TILE, HDIM), lambda h, t, *_: (t, h))

    def body(*refs):
        attend_kernel(tiles, wins, len(key_parts), *refs)

    operands = (query, *key_parts, *value_parts)
    return pl.pallas_call(
        body,
        grid_spec=pltpu.PrefetchScalarGridSpec(
            num_scalar_prefetch=2,
            grid=(heads, tiles // STEP),
            in_specs=[stepped, *(column(array) for array in operands[1:])],
            out_specs=stepped,
            scratch_shapes=[pltpu.VMEM((window, TILE, HDIM), jnp.bfloat16)] * 2,
        ),
        out_shape=jax.ShapeDtypeStruct(query.shape, jnp.bfloat16),
        compiler_params=pltpu.CompilerParams(vmem_limit_bytes=48 * 1024 * 1024),
        cost_estimate=pl.CostEstimate(
            flops=4 * rows * wins * TILE * width,
            bytes_accessed=2 * sum(array.size for array in operands) + 2 * query.size,
            transcendentals=rows * wins * TILE * heads,
        ),
    )(index, penalty, *operands)


def halo(own, hop):
    reach = REACH * TILE
    lower = shifted(own[own.shape[0] - reach :], "blk", hop)
    upper = shifted(own[:reach], "blk", -hop)
    return [lower, own, upper]


def general_shards(queries, keys, values, q_gain, k_gain, slopes, out_weight, kv_tiles, tile_frame):
    groups, blocks = lax.axis_size("head"), lax.axis_size("blk")
    position, group = lax.axis_index("blk"), lax.axis_index("head")
    hop = TEAM // groups
    member = lax.rem(position, hop)
    teams = [
        [head * blocks + first + inner for inner in range(hop) for head in range(groups)]
        for first in range(0, blocks, hop)
    ]
    lines = [list(range(first, first + hop)) for first in range(0, blocks, hop)]
    length, features = values.shape[1:]
    narrow = features // TEAM

    def to_heads(rows):
        parts = rows.reshape(length, groups, hop, narrow).transpose(2, 1, 0, 3)
        parts = lax.all_to_all(
            parts.reshape(TEAM, length, narrow),
            ("head", "blk"),
            split_axis=0,
            concat_axis=0,
            axis_index_groups=teams,
            tiled=True,
        )
        return parts.reshape(TEAM * length, narrow)

    full_columns = lax.all_gather(out_weight, "blk", axis=1, tiled=True)
    value_own = to_heads(values[0])
    key_own = to_heads(rms_norm(keys[0], k_gain))
    value_parts = halo(value_own, hop)
    query_normed = rms_norm(queries[0], q_gain * (LOG2E * HDIM ** (-0.5)))
    query_normed, value_parts[0], value_parts[2] = lax.optimization_barrier(
        (query_normed, value_parts[0], value_parts[2])
    )
    query_own = to_heads(query_normed)
    tiles = query_own.shape[0] // TILE
    key_parts = halo(key_own, hop)

    start = position // hop * tiles
    listed = lax.dynamic_slice_in_dim(kv_tiles, start, tiles, 0)
    own_frames = lax.dynamic_slice_in_dim(tile_frame, start, tiles, 0)
    gap = jnp.abs(own_frames[:, None] - jnp.take(tile_frame, listed, axis=0)).astype(jnp.float32)
    heads = narrow // HDIM
    own_slopes = lax.dynamic_slice_in_dim(slopes, member * heads, heads, 0)
    penalty = (own_slopes * LOG2E)[:, None] * gap.reshape(1, -1)
    index = (listed - (start - REACH)).reshape(-1)
    attended = attend(query_own, key_parts, value_parts, index, penalty.reshape(-1))
    attended = lax.all_to_all(
        attended.reshape(hop, groups * length, narrow),
        "blk",
        split_axis=0,
        concat_axis=0,
        axis_index_groups=lines,
        tiled=True,
    )
    attended = attended.transpose(1, 0, 2).reshape(groups * length, hop * narrow)

    rows = attended.shape[0] // groups
    width = full_columns.shape[1] // CHUNKS

    def partial(owner, chunk):
        return jnp.dot(
            lax.dynamic_slice_in_dim(attended, owner * rows, rows, 0),
            full_columns[:, chunk * width : (chunk + 1) * width],
            preferred_element_type=jnp.float32,
        ).astype(jnp.bfloat16)

    arrived = []
    for chunk in range(CHUNKS):
        arrived.append(
            [
                lax.ppermute(
                    partial(lax.rem(group + step, groups), chunk),
                    "head",
                    [(source, (source + step) % groups) for source in range(groups)],
                )
                for step in range(1, groups)
            ]
        )
    mixed = []
    for chunk in range(CHUNKS):
        floats = partial(group, chunk).astype(jnp.float32)
        for term in arrived[chunk]:
            floats = floats + term.astype(jnp.float32)
        mixed.append(floats.astype(jnp.bfloat16))
    return jnp.concatenate(mixed, axis=1)[None]


def shards(*arrays):
    queries, out_weight = arrays[0], arrays[6]
    rows = queries.shape[1]
    if lax.axis_size("head") == 2 and lax.axis_size("blk") % LINE == 0 and rows == TILE:
        if out_weight.shape[1] % HDIM == HDIM // 2:
            return fused_shards(*arrays)
    return general_shards(*arrays)


def solution(mesh):
    placed = (
        P("head", "blk", None),
        P("head", "blk", None),
        P("head", "blk", None),
        P(),
        P(),
        P("head"),
        P("head", "blk"),
        P(),
        P(),
    )
    return jax.shard_map(
        shards, mesh=mesh, in_specs=placed, out_specs=P("head", "blk", None), check_vma=False
    )
```

profile of v0, /device:TPU:9, one launch (start us, length us, event | category | flops | bytes accessed | tf_op | source)
XLA Modules:
  0.0 393.9 jit_solution(17019175859110810283)
XLA Ops:
  0.0 0.0 copy-start
  0.0 0.0 copy-start.1
  0.0 0.8 dynamic-slice_multiply_fusion
  0.8 0.7 dynamic_slice.11
  1.5 0.0 copy-done
  1.5 0.1 constant_dynamic-slice_fusion
  1.6 0.1 copy.16
  1.7 0.1 reshape.41
  1.7 0.0 copy-done.1
  1.8 0.0 copy-start.2
  1.8 0.7 gather_fusion
  2.5 0.1 reshape.40
  2.5 0.1 abs_convert_fusion
  2.6 0.1 convert_element_type.15
  2.7 0.7 reshape.38.refs_0_
  3.4 0.1 broadcast_multiply_fusion.1
  3.4 0.7 mul.38.refs_1_
  4.1 0.0 copy-done.2
  4.1 0.6 broadcast_multiply_fusion
  4.7 3.6 copy.14
  8.3 2.6 pad_select_fusion.refs_7_
  10.9 378.7 %shard_map.91 = bf16[1,384,5120]{2,1,0:T(8,128)(2,1)} custom-call(s32[32]{0:T(128)} %reshape.38.refs_0_, f32[160]{0:T(256)} %mul.38.refs_1_, f32[1,5120]{1,0:T(1,128)} %bitcast.2, f32[1,5120]{1,0:T(1,128)} %bitcast.3, bf16[1,384,5120]{2,1,0:T(8,128)(2,1)} %refs_4_.1, bf16[1,384,5120]{2,1,0:T(8,128)(2,1)} %refs_5_.1, bf16[1,384,5120]{2,1,0:T(8,128)(2,1)} %refs_6_.1, ...), custom_call_target="tpu_custom_call" | custom-call | flops 32212254720 | bytes 17367040 | tf_op jit(solution)/shard_map/pallas_call | solution.py:381
  389.6 4.3 %copy.18 = bf16[1,384,5120]{2,1,0:T(8,128)(2,1)} copy(bf16[1,384,5120]{2,1,0:T(8,128)(2,1)} %shard_map.91) | data formatting | bytes 7864320
  (2 shorter events, 0.0 us)
Async XLA Ops:
  0.0 1.5 copy-start
  0.0 1.7 copy-start.1
  1.8 2.3 copy-start.2
where the time goes:
time: 394 us
  Pallas kernels  379 us (96%)
  local copies, waits for them, and re-layouts  11 us (3%)
  other arithmetic  4.09 us (1%)
    pallas_call x1, Pallas kernels, fused_shards(): pl.pallas_call(body, in_specs=[smem, smem, vmem, vmem, anywhere, anywhere...  379 us
    unnamed x9, local copies, waits for them, and re-layouts  7.99 us

commit v1 on v0

--- a/solution.py
+++ b/solution.py
@@ -15,7 +15,6 @@
 TEAM = 8
 STEP = 2
 LINE = 4
-PIECES = 5
 NORM_ROWS = 64
 NORM_GROUP = 16
 MESH = pl.DeviceIdType.MESH
@@ -23,14 +22,12 @@
 VMEM_LIMIT = 60 * 1024 * 1024
 
 
-def fused_kernel(sizes, index_ref, penalty_ref, q_gain_ref, k_gain_ref, q_ref, k_ref, v_ref, w_ref, out_ref, *scratch):
+def fused_kernel(sizes, near_ref, frame_ref, slope_ref, q_gain_ref, k_gain_ref, q_ref, k_ref, v_ref, w_ref, out_ref, *scratch):
     planes, hpd, length, pair = sizes
     wins = REACH + 1
     slabs = TEAM * hpd
     per_tile = pair // HDIM
-    frame = w_ref.shape[1]
-    base = frame - HDIM
-    inner = w_ref.shape[0]
+    narrow, inner = w_ref.shape
     key_wins, value_wins = scratch[:hpd], scratch[hpd : 2 * hpd]
     (queries, keys_n, queries_n, gathered, weight, arrived, raw) = scratch[2 * hpd : 2 * hpd + 7]
     (
@@ -88,31 +85,75 @@
         pl.semaphore_signal(barrier, inc=1, device_id=device(x, zz, m), device_id_type=MESH)
     pl.semaphore_wait(barrier, len(mates) + len(planes_off))
 
-    rail = pl.ds(pl.multiple_of(c * frame, HDIM), frame)
+    rail = pl.ds(pl.multiple_of(c * narrow, HDIM // 2), narrow)
+    rest = pl.ds(pl.multiple_of((1 - c) * narrow, HDIM // 2), narrow)
     sibling = device(x, z, y * 2 + 1 - c)
 
-    def weight_piece(piece):
-        rows = pl.ds(piece * (inner // PIECES), inner // PIECES)
-        for k, zz in enumerate(planes_off):
-            remote(w_ref.at[rows], weight.at[z, rows, rail], w_send.at[k], w_recv.at[z * 2 + c], device(x, zz, m))
-
-    def weight_forward(zz):
-        wait(weight.at[zz, :, rail], w_recv.at[zz * 2 + c])
-        remote(weight.at[zz, :, rail], weight.at[zz, :, rail], w_send.at[planes], w_recv.at[zz * 2 + c], sibling)
-
-    local(w_ref, weight.at[z, :, rail], w_local)
-    remote(w_ref, weight.at[z, :, rail], w_send.at[planes - 1], w_recv.at[z * 2 + c], sibling)
-
-    def scatter(kind, h, source, window, at):
-        for xx, mm in mates:
-            head = (xx * LINE + mm) * hpd + h
-            remote(source(head), window.at[at], qkv_send.at[kind], qkv_recv.at[kind, h], device(xx, z, mm))
-        local(source((x * LINE + m) * hpd + h), window.at[at], qkv_local.at[kind, h])
+    def weight_send(block, source, step):
+        there = weight.at[block, rail]
+        arrival = w_recv.at[block * 2 + c]
+        if step >= 0:
+
+            @pl.when(z < planes - 1)
+            def _():
+                remote(source, there, w_send.at[step, 0], arrival, device(x, z + 1, m))
+
+        if step <= 0:
+
+            @pl.when(z > 0)
+            def _():
+                remote(source, there, w_send.at[-step, 1], arrival, device(x, z - 1, m))
+
+        remote(source, there, w_send.at[abs(step), 2 + (step < 0)], arrival, sibling)
+
+    def weight_forward(step):
+        for sign in (1, -1):
+
+            @pl.when(z >= step if sign > 0 else z < planes - step)
+            def _():
+                block = z - sign * step
+                wait(weight.at[block, rail], w_recv.at[block * 2 + c])
+                weight_send(block, weight.at[block, rail], sign * step)
+
+    def weight_left():
+        @pl.when(z < planes - 1)
+        def _():
+            wait(w_ref, w_send.at[0, 0])
+
+        @pl.when(z > 0)
+        def _():
+            wait(w_ref, w_send.at[0, 1])
+
+        wait(w_ref, w_send.at[0, 2])
+        for step in range(1, planes):
+            for way in range(2):
+                here = z >= step if way == 0 else z < planes - step
+                onward = z < planes - 1 if way == 0 else z > 0
+
+                @pl.when(here)
+                def _():
+                    wait(w_ref, w_send.at[step, 2 + way])
+
+                @pl.when(here & onward)
+                def _():
+                    wait(w_ref, w_send.at[step, way])
+
+    local(w_ref, weight.at[z, rail], w_local)
+    weight_send(z, w_ref, 0)
+
+    def scatter(kind, h, source, window, at, side=None):
+        for (xx, mm), (dx, _, _) in zip(mates, FLIPS):
+            if side is None or side == dx:
+                head = (xx * LINE + mm) * hpd + h
+                slot = kind + 1 if side == 0 else kind
+                remote(source(head), window.at[at], qkv_send.at[slot], qkv_recv.at[slot, h], device(xx, z, mm))
+        if side != 1:
+            local(source((x * LINE + m) * hpd + h), window.at[at], qkv_local.at[kind, h])
 
     for h in range(hpd):
         scatter(0, h, lambda head: v_ref.at[0, :, lanes(head)], value_wins[h], REACH + me)
 
-    def normed(source, gain_ref, target):
+    def normed(source, gain_ref, scale, target):
         steps = length // NORM_ROWS
 
         def chunk(step, slot):
@@ -136,21 +177,19 @@
             def _(group):
                 floats = raw[slot, pl.ds(group * NORM_GROUP, NORM_GROUP), :].astype(jnp.float32)
                 factor = lax.rsqrt(jnp.mean(floats * floats, axis=-1, keepdims=True) + 1e-06)
-                rows = (floats * factor * gain_ref[...]).astype(jnp.bfloat16)
+                rows = (floats * (factor * scale) * gain_ref[...]).astype(jnp.bfloat16)
                 at = pl.ds(step * NORM_ROWS + group * NORM_GROUP, NORM_GROUP)
                 for slab in range(slabs):
                     target[slab, at, :] = rows[:, slab * HDIM : (slab + 1) * HDIM]
 
-    normed(k_ref, k_gain_ref, keys_n)
-    normed(q_ref, q_gain_ref, queries_n)
+    normed(k_ref, k_gain_ref, 1.0, keys_n)
+    normed(q_ref, q_gain_ref, LOG2E * HDIM ** (-0.5), queries_n)
     for h in range(hpd):
         scatter(1, h, lambda head: keys_n.at[head], key_wins[h], REACH + me)
-        scatter(2, h, lambda head: queries_n.at[head], queries.at[h], me)
-    weight_piece(0)
+        scatter(2, h, lambda head: queries_n.at[head], queries.at[h], me, 1)
 
     def landed(kind, h, window, first):
-        own = window.at[pl.ds(first, TEAM - 1)]
-        wait(own, qkv_recv.at[kind, h])
+        wait(window.at[pl.ds(first, TEAM - 1)], qkv_recv.at[kind, h])
         wait(window.at[first], qkv_local.at[kind, h])
 
     top = REACH + TEAM
@@ -189,33 +228,37 @@
             def _():
                 wait(window.at[pl.ds(top, REACH)], halo_recv.at[kind, 1, h])
 
-    def attend(h):
-        halo_landed(h)
-
-        @pl.loop(0, TEAM)
-        def _(i):
-            part, mm = i // LINE, i % LINE
+    def penalty(h, tile, near):
+        gap = jnp.abs(frame_ref[tile] - frame_ref[near]).astype(jnp.float32)
+        return slope_ref[m * hpd + h] * LOG2E * gap
+
+    def attend(part, h):
+        @pl.loop(0, LINE)
+        def _(mm):
             tile = mm * 2 + (x + 1 - part) % 2
+            at = z * TEAM + tile
+            nears = [near_ref[at * wins + win] for win in range(wins)]
+            slots = [jnp.clip(near - (z * TEAM - REACH), 0, TEAM + 2 * REACH - 1) for near in nears]
             query = queries[h, tile]
             scores = []
             largest = None
             for win in range(wins):
-                near = key_wins[h][index_ref[tile * wins + win]]
+                near = key_wins[h][slots[win]]
                 score = lax.dot_general(
                     query, near, (((1,), (1,)), ((), ())), preferred_element_type=jnp.float32
                 )
-                penalty = penalty_ref[(h * TEAM + tile) * wins + win]
-                most = jnp.max(score, axis=-1, keepdims=True) - penalty
+                less = penalty(h, at, nears[win])
+                most = jnp.max(score, axis=-1, keepdims=True) - less
                 largest = most if largest is None else jnp.maximum(largest, most)
-                scores.append((score, penalty))
+                scores.append((score, less))
             total = jnp.zeros((length, 1), jnp.float32)
             summed = jnp.zeros((length, HDIM), jnp.float32)
-            for win, (score, penalty) in enumerate(scores):
-                share = jnp.exp2(score - (largest + penalty))
+            for win, (score, less) in enumerate(scores):
+                share = jnp.exp2(score - (largest + less))
                 total += jnp.sum(share, axis=-1, keepdims=True)
                 summed += jnp.dot(
                     share.astype(jnp.bfloat16),
-                    value_wins[h][index_ref[tile * wins + win]],
+                    value_wins[h][slots[win]],
                     preferred_element_type=jnp.float32,
                 )
             queries[h, tile] = (summed / total).astype(jnp.bfloat16)
@@ -235,21 +278,26 @@
 
     for h in range(hpd):
         spread(0, h, value_wins[h])
-    for piece in range(1, 3):
-        weight_piece(piece)
     for h in range(hpd):
         spread(1, h, key_wins[h])
-        landed(2, h, queries.at[h], 0)
-        if h == 1:
-            weight_piece(3)
+        wait(queries.at[h, pl.ds(0, LINE)], qkv_recv.at[2, h])
         if h == 2:
-            weight_piece(4)
+            weight_forward(1)
         if h > 0:
-            attend(h - 1)
-    attend(hpd - 1)
+            halo_landed(h - 1)
+            attend(0, h - 1)
+    halo_landed(hpd - 1)
+    attend(0, hpd - 1)
+    for h in range(hpd):
+        scatter(2, h, lambda head: queries_n.at[head], queries.at[h], me, 0)
+    weight_forward(2)
+
+    def attend_own(h):
+        wait(queries.at[h, pl.ds(0, LINE - 1)], qkv_recv.at[3, h])
+        wait(queries.at[h, 0], qkv_local.at[2, h])
+        attend(1, h)
 
     wait(keys_n.at[pl.ds(0, (TEAM - 1) * hpd)], qkv_send.at[1])
-    wait(queries_n.at[pl.ds(0, (TEAM - 1) * hpd)], qkv_send.at[2])
 
     def near_plane(k):
         if k == 0:
@@ -259,16 +307,15 @@
             return (high + k // 2) % 2 * 2 + (low + k % 2) % 2
         return (z + k) % planes
 
-    def project(part, row, zz):
-        own = gathered[part * 2 + row]
-        for start, width in ((0, base), (base, 2 * HDIM), (base + 2 * HDIM, base)):
-            product = jnp.dot(own, weight[zz, :, start : start + width], preferred_element_type=jnp.float32)
-            if start == base:
-                yield base // HDIM, product[:, :HDIM] + product[:, HDIM:]
-            else:
-                first = start // HDIM if start < base else start // HDIM - 1
-                for at in range(width // HDIM):
-                    yield first + at, product[:, at * HDIM : (at + 1) * HDIM]
+    def project(part, zz, first, width):
+        return lax.dot_general(
+            gathered[part * 2 : part * 2 + 2].reshape(2 * length, inner),
+            weight[zz, first : first + width, :],
+            (((1,), (1,)), ((), ())),
+            preferred_element_type=jnp.float32,
+        )
+
+    spans = [(first, min(2 * HDIM, pair - first)) for first in range(0, pair, 2 * HDIM)]
 
     def attended_landed(part):
         wait(keys_n.at[pl.ds(0, 2 * (LINE - 1) * hpd)], att_recv.at[part])
@@ -276,20 +323,21 @@
 
     attended_landed(0)
     per_plane = 2 * per_tile
+    turns = [k * hpd // planes for k in range(planes + 1)]
     for k in range(planes):
         zz = near_plane(k)
         if k == 0:
-            wait(weight.at[zz, :, rail], w_local)
-        else:
-            weight_forward(zz)
-        rest = pl.ds(pl.multiple_of((1 - c) * frame, HDIM), frame)
-        wait(weight.at[zz, :, rest], w_recv.at[zz * 2 + 1 - c])
-
-        @pl.loop(0, 2)
-        def _(row):
-            for slab, product in project(0, row, zz):
-                keys_n[k * per_plane + row * per_tile + slab] = product.astype(jnp.bfloat16)
-
+            wait(weight.at[zz, rail], w_local)
+        if k == planes - 1:
+            for step in range(3, planes):
+                weight_forward(step)
+        wait(weight.at[zz, rest], w_recv.at[zz * 2 + 1 - c])
+        for first, width in spans:
+            product = project(0, zz, first, width).astype(jnp.bfloat16)
+            for row in range(2):
+                for at in range(width // HDIM):
+                    slab = k * per_plane + row * per_tile + first // HDIM + at
+                    keys_n[slab] = product[row * length : (row + 1) * length, at * HDIM : (at + 1) * HDIM]
         remote(
             keys_n.at[pl.ds(k * per_plane, per_plane)],
             arrived.at[k],
@@ -297,29 +345,39 @@
             x_recv.at[k],
             device(1 - x, z, m),
         )
-
+        for h in range(turns[k], turns[k + 1]):
+            attend_own(h)
+
+    wait(queries_n.at[pl.ds(0, LINE * hpd)], qkv_send.at[2])
+    wait(queries_n.at[pl.ds(0, (LINE - 1) * hpd)], qkv_send.at[3])
     attended_landed(1)
     for k in range(planes):
         zz = near_plane(k)
         wait(arrived.at[k], x_recv.at[k])
-
-        @pl.loop(0, 2)
-        def _(turn):
-            row = (turn + 1 - y) % 2
-            for slab, product in project(1, row, zz):
-                floats = product + arrived[k, row * per_tile + slab].astype(jnp.float32)
-                queries_n[k * per_plane + row * per_tile + slab] = floats.astype(jnp.bfloat16)
-            for slab in range(per_tile):
-                source = queries_n.at[k * per_plane + row * per_tile + slab]
-                there = out_ref.at[0, :, lanes((zz * 2 + y) * per_tile + slab)]
-
-                @pl.when(row == y)
-                def _():
-                    local(source, there, out_local)
-
-                @pl.when(row != y)
-                def _():
-                    remote(source, there, y_send, y_recv, device(x, z, (1 - y) * 2 + c))
+        for first, width in spans:
+            product = project(1, zz, first, width)
+            for row in range(2):
+                for at in range(width // HDIM):
+                    lane = first // HDIM + at
+                    slab = k * per_plane + row * per_tile + lane
+                    floats = product[row * length : (row + 1) * length, at * HDIM : (at + 1) * HDIM]
+                    floats = floats + arrived[k, row * per_tile + lane].astype(jnp.float32)
+                    queries_n[slab] = floats.astype(jnp.bfloat16)
+
+            @pl.loop(0, 2)
+            def _(row):
+                for at in range(width // HDIM):
+                    lane = first // HDIM + at
+                    source = queries_n.at[k * per_plane + row * per_tile + lane]
+                    there = out_ref.at[0, :, lanes((zz * 2 + y) * per_tile + lane)]
+
+                    @pl.when(row == y)
+                    def _():
+                        local(source, there, out_local)
+
+                    @pl.when(row != y)
+                    def _():
+                        remote(source, there, y_send, y_recv, device(x, z, (1 - y) * 2 + c))
 
     half = planes * per_tile
     wait(queries_n.at[pl.ds(0, half)], y_recv)
@@ -330,9 +388,7 @@
     wait(keys_n.at[pl.ds(0, (TEAM - 1) * hpd)], qkv_send.at[0])
     wait(keys_n, att_send.at[0])
     wait(keys_n.at[pl.ds(0, LINE * hpd)], att_send.at[1])
-    for k in range(planes):
-        wait(w_ref, w_send.at[k])
-    wait(weight.at[pl.ds(0, planes - 1), :, rail], w_send.at[planes])
+    weight_left()
     for h in range(hpd):
         for kind, window in ((0, value_wins[h]), (1, key_wins[h])):
 
@@ -347,26 +403,11 @@
 
 def fused_shards(queries, keys, values, q_gain, k_gain, slopes, out_weight, kv_tiles, tile_frame):
     blocks = lax.axis_size("blk")
-    position = lax.axis_index("blk")
-    planes, member = blocks // LINE, lax.rem(position, LINE)
+    planes = blocks // LINE
     length, features = values.shape[1:]
     hpd = features // (TEAM * HDIM)
     inner, narrow = out_weight.shape
-    pair, frame = 2 * narrow, narrow + HDIM // 2
-
-    start = position // LINE * TEAM
-    listed = lax.dynamic_slice_in_dim(kv_tiles, start, TEAM, 0)
-    own_frames = lax.dynamic_slice_in_dim(tile_frame, start, TEAM, 0)
-    gap = jnp.abs(own_frames[:, None] - jnp.take(tile_frame, listed, axis=0)).astype(jnp.float32)
-    own_slopes = lax.dynamic_slice_in_dim(slopes, member * hpd, hpd, 0)
-    penalty = (own_slopes * LOG2E)[:, None] * gap.reshape(1, -1)
-    index = (listed - (start - REACH)).reshape(-1)
-
-    framed = jnp.where(
-        position % 2 == 0,
-        jnp.pad(out_weight, ((0, 0), (0, HDIM // 2))),
-        jnp.pad(out_weight, ((0, 0), (HDIM // 2, 0))),
-    )
+    pair = 2 * narrow
 
     def body(*refs):
         fused_kernel((planes, hpd, length, pair), *refs)
@@ -380,7 +421,7 @@
     rows = TEAM * length
     return pl.pallas_call(
         body,
-        in_specs=[smem, smem, vmem, vmem, anywhere, anywhere, anywhere, anywhere],
+        in_specs=[smem, smem, smem, vmem, vmem, anywhere, anywhere, anywhere, anywhere],
         out_specs=anywhere,
         out_shape=jax.ShapeDtypeStruct((1, length, narrow * blocks), half),
         scratch_shapes=[window] * (2 * hpd)
@@ -389,16 +430,16 @@
             pltpu.VMEM((slabs, length, HDIM), half),
             pltpu.VMEM((slabs, length, HDIM), half),
             pltpu.VMEM((4, length, inner), half),
-            pltpu.VMEM((planes, inner, 2 * frame), half),
+            pltpu.VMEM((planes, pair, inner), half),
             pltpu.VMEM((planes, 2 * pair // HDIM, length, HDIM), half),
             pltpu.VMEM((2, NORM_ROWS, features), half),
             dma((2,)),
-            dma((3,)),
-            dma((3, hpd)),
+            dma((4,)),
+            dma((4, hpd)),
             dma((3, hpd)),
             dma((2, 2, hpd)),
             dma((2, 2, hpd)),
-            dma((planes + 1,)),
+            dma((planes, 4)),
             dma((2 * planes,)),
             dma,
             dma((2,)),
@@ -419,14 +460,15 @@
             transcendentals=rows * (REACH + 1) * TILE * hpd,
         ),
     )(
-        index,
-        penalty.reshape(-1),
-        (q_gain * (LOG2E * HDIM ** (-0.5)))[None],
+        kv_tiles.reshape(-1),
+        tile_frame,
+        slopes,
+        q_gain[None],
         k_gain[None],
         queries,
         keys,
         values,
-        framed,
+        out_weight.T,
     )
 
 
@@ -617,7 +659,7 @@
     queries, out_weight = arrays[0], arrays[6]
     rows = queries.shape[1]
     if lax.axis_size("head") == 2 and lax.axis_size("blk") % LINE == 0 and rows == TILE:
-        if out_weight.shape[1] % HDIM == HDIM // 2:
+        if 2 * out_weight.shape[1] % HDIM == 0:
             return fused_shards(*arrays)
     return general_shards(*arrays)
 

time: 394 us -> 280 us (0.71)
  Pallas kernels: 379 us -> 272 us
  local copies, waits for them, and re-layouts: 11 us -> 5.67 us
  other arithmetic: 4.09 us -> 0 us
    pallas_call x1, Pallas kernels: 379 us -> 272 us  [fused_shards(): pl.pallas_call(body, in_specs=[smem, smem, smem, vmem, vmem, anywhere, an...]
    unnamed x9 -> x2, local copies, waits for them, and re-layouts: 7.99 us -> 5.05 us
where the time goes in v1:
time: 280 us; the launch traced here: 278 us
  Pallas kernels  272 us (97%)
  local copies, waits for them, and re-layouts  5.67 us (2%)
    pallas_call x1, Pallas kernels, fused_shards(): pl.pallas_call(body, in_specs=[smem, smem, smem, vmem, vmem, anywhere, an...  272 us

profile of v1, /device:TPU:9, one launch (start us, length us, event | category | flops | bytes accessed | tf_op | source)
XLA Modules:
  0.0 277.8 jit_solution(1366937134468218615)
XLA Ops:
  0.0 0.8 copy.11
  0.8 0.6 reshape.3.refs_0_
  1.4 272.1 %shard_map.91 = bf16[1,384,5120]{2,1,0:T(8,128)(2,1)} custom-call(s32[128]{0:T(128)} %reshape.3.refs_0_, s32[32]{0:T(128)} %refs_1_.1, f32[20]{0:T(128)} %refs_2_.1, f32[1,5120]{1,0:T(1,128)} %bitcast.4, f32[1,5120]{1,0:T(1,128)} %bitcast.5, bf16[1,384,5120]{2,1,0:T(8,128)(2,1)} %refs_5_.1, bf16[1,384,5120]{2,1,0:T(8,128)(2,1)} %refs_6_.1, ...), custom_call_target="tpu_custom_call" | custom-call | flops 32212254720 | bytes 17367040 | tf_op jit(solution)/shard_map/pallas_call | solution.py:422
  273.5 4.3 %copy.13 = bf16[1,384,5120]{2,1,0:T(8,128)(2,1)} copy(bf16[1,384,5120]{2,1,0:T(8,128)(2,1)} %shard_map.91) | data formatting | bytes 7864320

commit v2 on v1

--- a/solution.py
+++ b/solution.py
@@ -15,6 +15,7 @@
 TEAM = 8
 STEP = 2
 LINE = 4
+PIECES = 4
 NORM_ROWS = 64
 NORM_GROUP = 16
 MESH = pl.DeviceIdType.MESH
@@ -86,12 +87,16 @@
     pl.semaphore_wait(barrier, len(mates) + len(planes_off))
 
     rail = pl.ds(pl.multiple_of(c * narrow, HDIM // 2), narrow)
-    rest = pl.ds(pl.multiple_of((1 - c) * narrow, HDIM // 2), narrow)
     sibling = device(x, z, y * 2 + 1 - c)
 
-    def weight_send(block, source, step):
-        there = weight.at[block, rail]
-        arrival = w_recv.at[block * 2 + c]
+    portion = narrow // PIECES
+
+    def part_of(piece):
+        return pl.ds(pl.multiple_of(c * narrow + piece * portion, 16), portion)
+
+    def weight_along(block, source, step, piece):
+        there = weight.at[block, part_of(piece)]
+        arrival = w_recv.at[block * 2 + c, piece]
         if step >= 0:
 
             @pl.when(z < planes - 1)
@@ -104,16 +109,23 @@
             def _():
                 remote(source, there, w_send.at[-step, 1], arrival, device(x, z - 1, m))
 
-        remote(source, there, w_send.at[abs(step), 2 + (step < 0)], arrival, sibling)
-
-    def weight_forward(step):
+    def weight_across(block, source, step, piece):
+        there = weight.at[block, part_of(piece)]
+        remote(source, there, w_send.at[abs(step), 2 + (step < 0)], w_recv.at[block * 2 + c, piece], sibling)
+
+    def weight_own(piece):
+        weight_along(z, w_ref.at[pl.ds(piece * portion, portion)], 0, piece)
+
+    def weight_forward(step, piece):
         for sign in (1, -1):
 
             @pl.when(z >= step if sign > 0 else z < planes - step)
             def _():
                 block = z - sign * step
-                wait(weight.at[block, rail], w_recv.at[block * 2 + c])
-                weight_send(block, weight.at[block, rail], sign * step)
+                here = weight.at[block, part_of(piece)]
+                wait(here, w_recv.at[block * 2 + c, piece])
+                weight_along(block, here, sign * step, piece)
+                weight_across(block, here, sign * step, piece)
 
     def weight_left():
         @pl.when(z < planes - 1)
@@ -139,7 +151,10 @@
                     wait(w_ref, w_send.at[step, way])
 
     local(w_ref, weight.at[z, rail], w_local)
-    weight_send(z, w_ref, 0)
+    for piece in range(PIECES):
+        weight_across(z, w_ref.at[pl.ds(piece * portion, portion)], 0, piece)
+    weight_own(0)
+    weight_own(1)
 
     def scatter(kind, h, source, window, at, side=None):
         for (xx, mm), (dx, _, _) in zip(mates, FLIPS):
@@ -237,7 +252,7 @@
         def _(mm):
             tile = mm * 2 + (x + 1 - part) % 2
             at = z * TEAM + tile
-            nears = [near_ref[at * wins + win] for win in range(wins)]
+            nears = [near_ref[win, at] for win in range(wins)]
             slots = [jnp.clip(near - (z * TEAM - REACH), 0, TEAM + 2 * REACH - 1) for near in nears]
             query = queries[h, tile]
             scores = []
@@ -278,11 +293,14 @@
 
     for h in range(hpd):
         spread(0, h, value_wins[h])
+    waiting = [lambda piece=piece: weight_own(piece) for piece in range(2, PIECES)]
+    waiting += [lambda piece=piece: weight_forward(1, piece) for piece in range(PIECES)]
+    waiting.pop(0)()
     for h in range(hpd):
         spread(1, h, key_wins[h])
         wait(queries.at[h, pl.ds(0, LINE)], qkv_recv.at[2, h])
-        if h == 2:
-            weight_forward(1)
+        if waiting:
+            waiting.pop(0)()
         if h > 0:
             halo_landed(h - 1)
             attend(0, h - 1)
@@ -290,7 +308,10 @@
     attend(0, hpd - 1)
     for h in range(hpd):
         scatter(2, h, lambda head: queries_n.at[head], queries.at[h], me, 0)
-    weight_forward(2)
+    for step in waiting:
+        step()
+    for piece in range(PIECES // 2):
+        weight_forward(2, piece)
 
     def attend_own(h):
         wait(queries.at[h, pl.ds(0, LINE - 1)], qkv_recv.at[3, h])
@@ -328,10 +349,14 @@
         zz = near_plane(k)
         if k == 0:
             wait(weight.at[zz, rail], w_local)
-        if k == planes - 1:
-            for step in range(3, planes):
-                weight_forward(step)
-        wait(weight.at[zz, rest], w_recv.at[zz * 2 + 1 - c])
+        if k == 1:
+            for piece in range(PIECES // 2, PIECES):
+                weight_forward(2, piece)
+        if k >= 3:
+            for piece in range(PIECES):
+                weight_forward(k, piece)
+        for piece in range(PIECES):
+            wait(weight.at[zz, pl.ds(0, portion)], w_recv.at[zz * 2 + 1 - c, piece])
         for first, width in spans:
             product = project(0, zz, first, width).astype(jnp.bfloat16)
             for row in range(2):
@@ -440,7 +465,7 @@
             dma((2, 2, hpd)),
             dma((2, 2, hpd)),
             dma((planes, 4)),
-            dma((2 * planes,)),
+            dma((2 * planes, PIECES)),
             dma,
             dma((2,)),
             dma((2,)),
@@ -460,7 +485,7 @@
             transcendentals=rows * (REACH + 1) * TILE * hpd,
         ),
     )(
-        kv_tiles.reshape(-1),
+        kv_tiles.T,
         tile_frame,
         slopes,
         q_gain[None],
@@ -659,7 +684,7 @@
     queries, out_weight = arrays[0], arrays[6]
     rows = queries.shape[1]
     if lax.axis_size("head") == 2 and lax.axis_size("blk") % LINE == 0 and rows == TILE:
-        if 2 * out_weight.shape[1] % HDIM == 0:
+        if out_weight.shape[1] % (HDIM // 2) == 0:
             return fused_shards(*arrays)
     return general_shards(*arrays)
 

time: 280 us -> 269 us (0.961)
  Pallas kernels: 272 us -> 263 us
    pallas_call x1, Pallas kernels: 272 us -> 263 us  [fused_shards(): pl.pallas_call(body, in_specs=[smem, smem, smem, vmem, vmem, anywhere, an...]
where the time goes in v2:
time: 269 us; the launch traced here: 267 us
  Pallas kernels  263 us (98%)
  local copies, waits for them, and re-layouts  4.29 us (2%)
    pallas_call x1, Pallas kernels, fused_shards(): pl.pallas_call(body, in_specs=[smem, smem, smem, vmem, vmem, anywhere, an...  263 us

profile of v2, /device:TPU:9, one launch (start us, length us, event | category | flops | bytes accessed | tf_op | source)
XLA Modules:
  0.0 267.2 jit_solution(14494936294802741129)
XLA Ops:
  0.0 262.9 %shard_map.91 = bf16[1,384,5120]{2,1,0:T(8,128)(2,1)} custom-call(s32[4,32]{1,0:T(4,128)} %bitcast.7, s32[32]{0:T(128)} %refs_1_.1, f32[20]{0:T(128)} %refs_2_.1, f32[1,5120]{1,0:T(1,128)} %bitcast.5, f32[1,5120]{1,0:T(1,128)} %bitcast.6, bf16[1,384,5120]{2,1,0:T(8,128)(2,1)} %refs_5_.1, bf16[1,384,5120]{2,1,0:T(8,128)(2,1)} %refs_6_.1, ...), custom_call_target="tpu_custom_call" | custom-call | flops 32212254720 | bytes 17367040 | tf_op jit(solution)/shard_map/pallas_call | solution.py:447
  262.9 4.3 %copy.11 = bf16[1,384,5120]{2,1,0:T(8,128)(2,1)} copy(bf16[1,384,5120]{2,1,0:T(8,128)(2,1)} %shard_map.91) | data formatting | bytes 7864320

commit v3 on v2

--- a/solution.py
+++ b/solution.py
@@ -20,7 +20,7 @@
 NORM_GROUP = 16
 MESH = pl.DeviceIdType.MESH
 FLIPS = ((1, 0, 0), (0, 1, 0), (1, 0, 1), (0, 1, 1), (1, 1, 0), (1, 1, 1), (0, 0, 1))
-VMEM_LIMIT = 60 * 1024 * 1024
+VMEM_LIMIT = 55 * 1024 * 1024
 
 
 def fused_kernel(sizes, near_ref, frame_ref, slope_ref, q_gain_ref, k_gain_ref, q_ref, k_ref, v_ref, w_ref, out_ref, *scratch):
@@ -440,15 +440,16 @@
     dma, half = pltpu.SemaphoreType.DMA, jnp.bfloat16
     slabs = TEAM * hpd
     anywhere = pl.BlockSpec(memory_space=pl.ANY)
+    far = pl.BlockSpec(memory_space=pltpu.HBM)
     smem = pl.BlockSpec(memory_space=pltpu.SMEM)
     vmem = pl.BlockSpec(memory_space=pltpu.VMEM)
     window = pltpu.VMEM((TEAM + 2 * REACH, length, HDIM), half)
     rows = TEAM * length
     return pl.pallas_call(
         body,
-        in_specs=[smem, smem, smem, vmem, vmem, anywhere, anywhere, anywhere, anywhere],
+        in_specs=[smem, smem, smem, vmem, vmem, far, far, far, far],
         out_specs=anywhere,
-        out_shape=jax.ShapeDtypeStruct((1, length, narrow * blocks), half),
+        out_shape=pltpu.VMEM((1, length, narrow * blocks), half),
         scratch_shapes=[window] * (2 * hpd)
         + [
             pltpu.VMEM((hpd, TEAM, length, HDIM), half),

time: 269 us -> 267 us (level)
  no operation moved by 1% of the time
where the time goes in v3:
time: 267 us; the launch traced here: 265 us
  Pallas kernels  263 us (99%)
    pallas_call x1, Pallas kernels, fused_shards(): pl.pallas_call(body, in_specs=[smem, smem, smem, vmem, vmem, far, far, fa...  263 us

profile of v3, /device:TPU:9, one launch (start us, length us, event | category | flops | bytes accessed | tf_op | source)
XLA Modules:
  0.0 264.7 jit_solution(15693085701214524243)
XLA Ops:
  0.0 262.8 %shard_map.91 = bf16[1,384,5120]{2,1,0:T(8,128)(2,1)S(1)} custom-call(s32[4,32]{1,0:T(4,128)} %bitcast.7, s32[32]{0:T(128)} %refs_1_.1, f32[20]{0:T(128)} %refs_2_.1, f32[1,5120]{1,0:T(1,128)} %bitcast.5, f32[1,5120]{1,0:T(1,128)} %bitcast.6, bf16[1,384,5120]{2,1,0:T(8,128)(2,1)} %refs_5_.1, bf16[1,384,5120]{2,1,0:T(8,128)(2,1)} %refs_6_.1, ...), custom_call_target="tpu_custom_call" | custom-call | flops 32212254720 | bytes 17367040 | tf_op jit(solution)/shard_map/pallas_call | solution.py:448
  262.8 1.9 copy.11

commit v4 on v3

--- a/solution.py
+++ b/solution.py
@@ -19,7 +19,7 @@
 NORM_ROWS = 64
 NORM_GROUP = 16
 MESH = pl.DeviceIdType.MESH
-FLIPS = ((1, 0, 0), (0, 1, 0), (1, 0, 1), (0, 1, 1), (1, 1, 0), (1, 1, 1), (0, 0, 1))
+FLIPS = ((0, 1, 0), (1, 1, 0), (0, 1, 1), (1, 1, 1), (1, 0, 0), (1, 0, 1), (0, 0, 1))
 VMEM_LIMIT = 55 * 1024 * 1024
 
 

time: 267 us -> 266 us (level)
  no operation moved by 1% of the time
where the time goes in v4:
time: 266 us; the launch traced here: 264 us
  Pallas kernels  263 us (99%)
    pallas_call x1, Pallas kernels, fused_shards(): pl.pallas_call(body, in_specs=[smem, smem, smem, vmem, vmem, far, far, fa...  263 us

profile of v4, /device:TPU:9, one launch (start us, length us, event | category | flops | bytes accessed | tf_op | source)
XLA Modules:
  0.0 264.5 jit_solution(6715895898285714580)
XLA Ops:
  0.0 262.5 %shard_map.91 = bf16[1,384,5120]{2,1,0:T(8,128)(2,1)S(1)} custom-call(s32[4,32]{1,0:T(4,128)} %bitcast.7, s32[32]{0:T(128)} %refs_1_.1, f32[20]{0:T(128)} %refs_2_.1, f32[1,5120]{1,0:T(1,128)} %bitcast.5, f32[1,5120]{1,0:T(1,128)} %bitcast.6, bf16[1,384,5120]{2,1,0:T(8,128)(2,1)} %refs_5_.1, bf16[1,384,5120]{2,1,0:T(8,128)(2,1)} %refs_6_.1, ...), custom_call_target="tpu_custom_call" | custom-call | flops 32212254720 | bytes 17367040 | tf_op jit(solution)/shard_map/pallas_call | solution.py:448
  262.5 1.9 copy.11

commit v5 on v4

--- a/solution.py
+++ b/solution.py
@@ -150,12 +150,6 @@
                 def _():
                     wait(w_ref, w_send.at[step, way])
 
-    local(w_ref, weight.at[z, rail], w_local)
-    for piece in range(PIECES):
-        weight_across(z, w_ref.at[pl.ds(piece * portion, portion)], 0, piece)
-    weight_own(0)
-    weight_own(1)
-
     def scatter(kind, h, source, window, at, side=None):
         for (xx, mm), (dx, _, _) in zip(mates, FLIPS):
             if side is None or side == dx:
@@ -167,6 +161,12 @@
 
     for h in range(hpd):
         scatter(0, h, lambda head: v_ref.at[0, :, lanes(head)], value_wins[h], REACH + me)
+
+    local(w_ref, weight.at[z, rail], w_local)
+    for piece in range(PIECES):
+        weight_across(z, w_ref.at[pl.ds(piece * portion, portion)], 0, piece)
+    weight_own(0)
+    weight_own(1)
 
     def normed(source, gain_ref, scale, target):
         steps = length // NORM_ROWS

time: 266 us -> 266 us (level)
  no operation moved by 1% of the time
where the time goes in v5:
time: 266 us; the launch traced here: 264 us
  Pallas kernels  263 us (99%)
    pallas_call x1, Pallas kernels, fused_shards(): pl.pallas_call(body, in_specs=[smem, smem, smem, vmem, vmem, far, far, fa...  263 us

profile of v5, /device:TPU:9, one launch (start us, length us, event | category | flops | bytes accessed | tf_op | source)
XLA Modules:
  0.0 264.4 jit_solution(936041354012532130)
XLA Ops:
  0.0 262.5 %shard_map.91 = bf16[1,384,5120]{2,1,0:T(8,128)(2,1)S(1)} custom-call(s32[4,32]{1,0:T(4,128)} %bitcast.7, s32[32]{0:T(128)} %refs_1_.1, f32[20]{0:T(128)} %refs_2_.1, f32[1,5120]{1,0:T(1,128)} %bitcast.5, f32[1,5120]{1,0:T(1,128)} %bitcast.6, bf16[1,384,5120]{2,1,0:T(8,128)(2,1)} %refs_5_.1, bf16[1,384,5120]{2,1,0:T(8,128)(2,1)} %refs_6_.1, ...), custom_call_target="tpu_custom_call" | custom-call | flops 32212254720 | bytes 17367040 | tf_op jit(solution)/shard_map/pallas_call | solution.py:448
  262.5 1.9 copy.11
